TPU v7x, 512 devices: a whole 4x8x8 slice. The times are simulated.
512 devices in a mesh: ctx: 64 (over y, x, z_hi), head: 8 (over z_lo, core).
Axes of the slice: x: 4, y: 8, z: 8 (z_hi: 2, z_lo: 4; z = z_hi * 4 + z_lo), core: 2. Of those that a mesh axis runs over, the one named last changes fastest.
Arguments:
- qkv: bfloat16 [32768, 3, 512], P(('ctx', 'head')), may hold values from -10 to 10
- w_out: bfloat16 [512, 1024], replicated, may hold values from -0.25 to 0.25
Outputs:
- mixed: bfloat16 [32768, 1024], P(('ctx', 'head'))
All inputs are finite; a program needn't handle non-finite values.
Results may differ from a plain program's by a relative error of at most 0.0095.
Values may be sent and summed in bfloat16 or wider, within the bound.
A program may use at most 64 MiB of HBM per device.

v0:
```python
import jax
import jax.numpy as jnp
from jax import lax
from jax.sharding import PartitionSpec as P

HEADS = 8


def make_attend(queries, local_heads, head_size):

    def attend_block(running, kv_block):
        key_count = kv_block.shape[0]
        keys_values = kv_block.reshape(key_count, 2, local_heads, head_size)
        scores = jnp.einsum(
            "fhd,khd->hfk", queries, keys_values[:, 0], preferred_element_type=jnp.float32
        ) * head_size ** (-0.5)
        highest, totals, accumulated = running
        newest = jnp.maximum(highest, jnp.max(scores, axis=2))
        factor = jnp.exp(highest - newest)
        weights = jnp.exp(scores - newest[:, :, None])
        totals = totals * factor + jnp.sum(weights, axis=2)
        accumulated = accumulated * factor[:, :, None] + jnp.einsum(
            "hfk,khd->hfd",
            weights.astype(jnp.bfloat16),
            keys_values[:, 1],
            preferred_element_type=jnp.float32,
        )
        return (newest, totals, accumulated)

    def attend(running, kv_piece, first_row):
        key_count = kv_piece.shape[0]
        stacked = kv_piece.reshape(key_count // 2048, 2048, kv_piece.shape[1])

        def step_fn(state_now, kv_block):
            return (attend_block(state_now, kv_block), None)

        running, unused = lax.scan(step_fn, running, stacked)
        return running

    return attend


def body(qkv, w_out):
    frames_here = qkv.shape[0]
    head_size = qkv.shape[2] // HEADS
    head_devices = lax.axis_size("head")
    local_heads = HEADS // head_devices
    spread_qkv = qkv.reshape(frames_here, 3, HEADS, head_size)
    grouped = lax.all_to_all(spread_qkv, "head", split_axis=2, concat_axis=0, tiled=True)
    queries = grouped[:, 0]
    kv_local = grouped[:, 1:].reshape(grouped.shape[0], 2 * local_heads * head_size)
    query_rows = queries.shape[0]
    attend = make_attend(queries, local_heads, head_size)
    initial = (
        jnp.full((local_heads, query_rows), -1e30, jnp.float32),
        jnp.zeros((local_heads, query_rows), jnp.float32),
        jnp.zeros((local_heads, query_rows, head_size), jnp.float32),
    )
    whole_kv = lax.all_gather(kv_local, "ctx", axis=0, tiled=True)
    finished = attend(initial, whole_kv, 0)
    highest, totals, accumulated = finished
    attended = (accumulated / totals[:, :, None]).astype(jnp.bfloat16)
    returned = lax.all_to_all(attended, "head", split_axis=1, concat_axis=0, tiled=True)
    projection = w_out.reshape(HEADS, head_size, w_out.shape[1])
    mixed = jnp.einsum("htd,hde->te", returned, projection, preferred_element_type=jnp.float32)
    return mixed.astype(jnp.bfloat16)


def solution(mesh):
    return jax.shard_map(
        body,
        mesh=mesh,
        in_specs=(P(("ctx", "head"), None, None), P()),
        out_specs=P(("ctx", "head"), None),
        check_vma=False,
    )
```

profile of v0, /device:TPU:1, one launch (start us, length us, event | category | flops | bytes accessed | tf_op | source)
XLA Modules:
  0.0 400.6 jit_solution(2547468611647760212)
XLA Ops:
  8.4 15.7 %all_to_all.30 = bf16[8,2,6144]{2,1,0:T(2,128)(2,1)S(1)} all-to-all(bf16[8,2,6144]{2,1,0:T(2,128)(2,1)S(1)} %reshape.59), channel_id=1, replica_groups=mesh['ctx'=64,'head'=8] {'head'}, dimensions={0} | all-to-all | bytes 393216 | tf_op jit(solution)/shard_map/all_to_all | solution.py:49
  25.8 215.5 %all-gather.2.cloned.1.call-done = bf16[32768,128]{0,1:T(8,128)(2,1)} async-done(((bf16[512,128]{0,1:T(8,128)(2,1)}), bf16[32768,128]{0,1:T(8,128)(2,1)}) %all-gather.2.cloned.1.call-update) | async-done | bytes 8388624 | tf_op jit(solution)/shard_map/all_gather | solution.py:59
  241.3 8.3 %copy.29 = bf16[16,16,8,2048]{3,2,0,1:T(8,128)(2,1)} copy(bf16[16,16,8,2048]{3,2,1,0:T(8,128)(2,1)} %bitcast.75) | data formatting | bytes 16777216 | tf_op jit(solution)/shard_map/reshape | solution.py:32
  249.6 129.5 %while.15 = (s32[]{:T(128)}, f32[1,512]{1,0:T(1,128)S(1)}, f32[1,512]{1,0:T(1,128)S(1)}, f32[1,512,64]{1,2,0:T(8,128)S(1)}, bf16[16,2048,128]{1,2,0:T(8,128)(2,1...) while((s32[]{:T(128)}, f32[1,512]{1,0:T(1,128)S(1)}, f32[1,512]{1,0:T(1,128)S(1)}, ...), condition=%wide.region_3.4_spmd.clone, body=%wide.region_0.3_spmd.clone.sunk | while | flops 276924928 | bytes 31293568 | solution.py:37
  250.6 2.7 multiply_reduce_fusion.2
  253.4 3.1 fusion.26
  258.7 2.7 multiply_reduce_fusion.2
  261.5 3.1 fusion.26
  266.8 2.7 multiply_reduce_fusion.2
  269.6 3.1 fusion.26
  274.9 2.7 multiply_reduce_fusion.2
  277.6 3.1 fusion.26
  283.0 2.7 multiply_reduce_fusion.2
  285.7 3.1 fusion.26
  291.1 2.7 multiply_reduce_fusion.2
  293.8 3.1 fusion.26
  299.2 2.7 multiply_reduce_fusion.2
  301.9 3.1 fusion.26
  307.3 2.7 multiply_reduce_fusion.2
  310.0 3.1 fusion.26
  318.1 3.1 fusion.26
  323.5 2.7 multiply_reduce_fusion.2
  326.2 3.1 fusion.26
  334.3 3.1 fusion.26
  342.4 3.1 fusion.26
  347.8 2.7 multiply_reduce_fusion.2
  350.5 3.1 fusion.26
  358.6 3.1 fusion.26
  363.9 2.7 multiply_reduce_fusion.2
  366.7 3.1 fusion.26
  374.8 3.1 fusion.26
  381.4 11.2 %all_to_all.31 = bf16[8,2,2048]{2,1,0:T(2,128)(2,1)S(1)} all-to-all(bf16[8,2,2048]{2,1,0:T(2,128)(2,1)S(1)} %reshape.61), channel_id=1, replica_groups=mesh['ctx'=64,'head'=8] {'head'}, dimensions={0} | all-to-all | bytes 131072 | tf_op jit(solution)/shard_map/all_to_all | solution.py:63
  (141 shorter events, 56.5 us)
Async XLA Ops:
  6.5 386.2 %copy-start = (bf16[512,1024]{1,0:T(8,128)(2,1)S(1)}, bf16[512,1024]{1,0:T(8,128)(2,1)}, u32[]{:S(2)}) copy-start(bf16[512,1024]{1,0:T(8,128)(2,1)} %param.5) | copy-start | bytes 3145732
  6.5 234.8 %all-gather.2.cloned.1.call-start = ((), (), s32[]{:S(2)}) async-start(), calls=%async_computation.2 | async-start | bytes 8519680 | tf_op jit(solution)/shard_map/all_gather | solution.py:59
  253.4 3.4 copy-start.1
  261.5 3.4 copy-start.1
  269.5 3.4 copy-start.1
  277.6 3.4 copy-start.1
  285.7 3.4 copy-start.1
  293.8 3.4 copy-start.1
  301.9 3.4 copy-start.1
  310.0 3.4 copy-start.1
  318.1 3.4 copy-start.1
  326.2 3.4 copy-start.1
  334.3 3.4 copy-start.1
  342.4 3.4 copy-start.1
  350.5 3.4 copy-start.1
  358.6 3.4 copy-start.1
  366.7 3.4 copy-start.1
  374.7 3.4 copy-start.1
Sparse Core Ops, SparseCore 0:
  25.8 215.4 all-gather.1
where the time goes:
time: 402 us; the launch traced here: 401 us
  waiting for transfers between devices  216 us (54%)
  matrix products  57.4 us (14%)
  other arithmetic  51.3 us (13%)
  local copies, waits for them, and re-layouts  35.2 us (9%)
  blocking collectives  26.9 us (7%)
  between operations  13.5 us (3%)
    all_gather x1, waiting for transfers between devices, body(): whole_kv = lax.all_gather(kv_local, 'ctx', axis=0, tiled=True)  216 us
    reduce_sum x16, other arithmetic, attend_block(): totals = totals * factor + jnp.sum(weights, axis=2)  49.5 us
    dot_general x16, matrix products, attend_block(): jnp.einsum('fhd,khd->hfk', queries, keys_values[:, 0], preferred_element_...  43.3 us
    dynamic_slice x16, local copies, waits for them, and re-layouts, attend(): running, unused = lax.scan(step_fn, running, stacked)  17.3 us
    all_to_all x1, blocking collectives, body(): lax.all_to_all(spread_qkv, 'head', split_axis=2, concat_axis=0, tiled=True)  15.7 us
    dot_general x16, matrix products, attend_block(): jnp.einsum('hfk,khd->hfd', weights.astype(jnp.bfloat16), keys_values[:, 1...  13.1 us
    all_to_all x1, blocking collectives, body(): lax.all_to_all(attended, 'head', split_axis=1, concat_axis=0, tiled=True)  11.2 us
    reshape x1, local copies, waits for them, and re-layouts, attend(): stacked = kv_piece.reshape(key_count // 2048, 2048, kv_piece.shape[1])  8.26 us
  transfers between devices with their start and end apart: 1, of which 1 were waited for; matrix products, arithmetic and copies ran while one was open for 0% of the time, Pallas kernels for 0%

commit v1 on v0

v1 whole, which is shorter than its diff:
```python
import functools

import jax
import jax.numpy as jnp
from jax import lax
from jax.experimental import pallas as pl
from jax.experimental.pallas import tpu as pltpu
from jax.sharding import PartitionSpec as P

MESH = pl.DeviceIdType.MESH
F32 = jnp.float32
BF16 = jnp.bfloat16
LOG2E = 1.4426950408889634

KEY_LEFT = ((0, 1), (1, 3), (3, 5), (5, 7))
KEY_RIGHT = ((0, 2), (2, 4), (4, 6), (6, 7))


def dot(a, b):
    return jnp.dot(a, b, preferred_element_type=F32)


def device(y, x, z, c):
    return ((y * 4 + x) * 2 + z // 4, (z % 4) * 2 + c)


def kernel(
    qkv_ref, w_hbm, out_ref,
    pieces, grouped, keys, values, queries, stationary, total, highest,
    part_out, stat_out, part_in, stat_in, back_out, back_in, w_vmem, rows,
    a2a_s, a2a_r, kv_s, kv_r, q_s, q_r, po_s, po_r, bk_s, bk_r, w_sem,
):
    ctx, head = lax.axis_index("ctx"), lax.axis_index("head")
    y, x, z, c = ctx // 8, (ctx // 2) % 4, (ctx % 2) * 4 + head // 2, head % 2

    def y_peer(k):
        return device((y + k) % 8, x, z, c)

    def xc_peer(n):
        pair = n // 2
        dx = pair + pair // 2 - 2 * (pair // 3)
        return device(y, (x + dx) % 4, z, (c + n % 2) % 2)

    def inverse(n):
        pair = n // 2
        return 2 * ((2 * pair) % 3 + 3 * (pair // 3)) + n % 2

    left, right = device(y, x, (z + 7) % 8, c), device(y, x, (z + 1) % 8, c)

    barrier = pltpu.get_barrier_semaphore()
    partners = [y_peer(k) for k in range(1, 8)] + [xc_peer(n) for n in range(1, 8)] + [left, right]
    for partner in partners:
        pl.semaphore_signal(barrier, inc=1, device_id=partner, device_id_type=MESH)

    w_copy = pltpu.make_async_copy(w_hbm, w_vmem, w_sem)
    w_copy.start()

    for t in range(3):
        rows[t] = qkv_ref[:, t, :]
        for h in range(8):
            cut = rows[t, :, 64 * h : 64 * h + 64]
            pieces[h, t] = jnp.concatenate([cut[:32], cut[32:]], axis=1)
    for n in range(8):
        values[n, :, 64:80, :] = jnp.ones((2, 16, 256), BF16)
    for i in range(16):
        stationary[i, 0, 64:, :] = jnp.zeros((64, 256), BF16)
        stationary[i, 1, :64, :] = jnp.zeros((64, 256), BF16)

    pl.semaphore_wait(barrier, len(partners))

    def spread(k, first, count, part):
        there = (y + k) % 8
        return pltpu.make_async_remote_copy(
            src_ref=pieces.at[there, pl.ds(first, count)],
            dst_ref=grouped.at[pl.ds(first, count), y],
            send_sem=a2a_s.at[k, part],
            recv_sem=a2a_r.at[k, part],
            device_id=y_peer(k),
            device_id_type=MESH,
        )

    kv_spread = [spread(k, 1, 2, 0) for k in (4, 3, 5, 2, 6, 1, 7)]
    q_spread = [spread(k, 0, 1, 1) for k in (4, 3, 5, 2, 6, 1, 7)]
    for copy in kv_spread + q_spread:
        copy.start()
    for t in range(3):
        grouped[t, y] = pieces[y, t]
    started = kv_spread + q_spread

    def send_keys(step, direction, keys_too, values_too):
        here, there = (KEY_LEFT, KEY_RIGHT)[direction][step]
        copies = []
        for part, ref, wanted in ((0, keys, keys_too), (1, values, values_too)):
            if wanted:
                cut = (lambda n: ref.at[n]) if part == 0 else (lambda n: ref.at[n, :, pl.ds(0, 64)])
                copies.append(
                    pltpu.make_async_remote_copy(
                        src_ref=cut(here),
                        dst_ref=cut(there),
                        send_sem=kv_s.at[step, direction, part],
                        recv_sem=kv_r.at[there, part],
                        device_id=(left, right)[direction],
                        device_id_type=MESH,
                    )
                )
        for copy in copies:
            copy.start()
        started.extend(copies)
        return copies

    for copy in kv_spread:
        copy.wait_recv()
    keys[0] = grouped[1].reshape(256, 128)
    turned = grouped[2].reshape(256, 128).astype(F32).T.astype(BF16)
    values[0, 0, :64] = turned[:64]
    values[0, 1, :64] = turned[64:]
    arriving = [send_keys(0, 0, True, True), send_keys(0, 1, True, True)]

    for copy in q_spread:
        copy.wait_recv()
    queries[0] = (grouped[0].reshape(256, 128).astype(F32) * 0.125).T.astype(BF16)

    q_copies = {}
    for n in (1, 2, 4, 3, 5, 6, 7):
        q_copies[n] = pltpu.make_async_remote_copy(
            src_ref=queries.at[0],
            dst_ref=queries.at[inverse(n)],
            send_sem=q_s.at[n],
            recv_sem=q_r.at[inverse(n)],
            device_id=xc_peer(n),
            device_id_type=MESH,
        )
        q_copies[n].start()
        started.append(q_copies[n])

    def take_queries(n):
        if n:
            q_copies[inverse(n)].wait_recv()
        for t in range(2):
            half = queries[n, 64 * t : 64 * t + 64, :]
            stationary[2 * n + t, 0, :64, :] = half
            stationary[2 * n + t, 1, 64:, :] = half

    def take_keys(step):
        nonlocal arriving
        for copies in arriving:
            for copy in copies:
                copy.wait_recv()
        if step < 3:
            last = step == 2
            arriving = [send_keys(step + 1, 0, True, not last), send_keys(step + 1, 1, not last, True)]

    def scores(i, n):
        found, top = [], []
        for t in range(2):
            pair = [dot(keys[n], stationary[2 * i + t, h]) * LOG2E for h in range(2)]
            top.append(jnp.maximum(*[jnp.max(s.reshape(32, 8, 256), axis=0) for s in pair]))
            found.append(pair)
        return found, top

    def weigh(i, n, found, top, first):
        for t in range(2):
            newest = jnp.max(top[t], axis=0, keepdims=True)
            if not first:
                before = highest[2 * i + t][:1]
                newest = jnp.maximum(before, newest)
                factor = jnp.exp2(before - newest)
            highest[2 * i + t] = jnp.broadcast_to(newest, (8, 256))
            added = sum(dot(values[n, h], jnp.exp2(found[t][h] - newest).astype(BF16)) for h in range(2))
            total[2 * i + t] = added if first else total[2 * i + t] * factor + added

    def attend(units):
        held = []
        for i, n, first in units:
            held.append((i, n, *scores(i, n), first))
            if len(held) > 1:
                weigh(*held.pop(0))
        weigh(*held.pop(0))

    take_queries(0)
    attend([(0, 0, True)])
    take_queries(1)
    attend([(1, 0, True)])
    take_keys(0)
    attend([(i, n, False) for i in (0, 1) for n in (1, 2)])
    take_queries(2)
    take_queries(3)

    @pl.loop(2, 4)
    def _(i):
        attend([(i, n, n == 0) for n in range(3)])

    take_keys(1)

    @pl.loop(0, 2)
    def _(i):
        attend([(2 * i + k, n, False) for k in (0, 1) for n in (3, 4)])

    take_queries(4)
    take_queries(5)

    @pl.loop(4, 6)
    def _(i):
        attend([(i, n, n == 0) for n in range(5)])

    take_keys(2)
    take_queries(6)
    take_queries(7)

    @pl.loop(6, 8)
    def _(i):
        attend([(i, n, n == 0) for n in range(5)])

    take_keys(3)

    def give_back(n):
        there = inverse(n)
        pairs = ((part_out, part_in), (stat_out, stat_in))
        return [
            pltpu.make_async_remote_copy(
                src_ref=mine.at[n],
                dst_ref=theirs.at[there],
                send_sem=po_s.at[n, k],
                recv_sem=po_r.at[there, k],
                device_id=xc_peer(n),
                device_id_type=MESH,
            )
            for k, (mine, theirs) in enumerate(pairs)
        ]

    @pl.loop(0, 8)
    def _(j):
        i = 7 - j
        attend([(i, n, False) for n in (5, 6, 7)])
        for t in range(2):
            whole = total[2 * i + t]
            sums = whole[64:65]
            part_out[i, 64 * t : 64 * t + 64, :] = (whole[:64] * (1.0 / sums)).astype(BF16)
            stat_out[i, 4 * t : 4 * t + 4, :] = jnp.broadcast_to(highest[2 * i + t][:1] + jnp.log2(sums), (4, 256))

        @pl.when(i != 0)
        def _():
            for copy in give_back(i):
                copy.start()

    for n in range(1, 8):
        for copy in give_back(inverse(n)):
            copy.wait_recv()
    mixed = []
    for t in range(2):
        stats = [stat_out[0, 4 * t : 4 * t + 1, :]] + [stat_in[n, 4 * t : 4 * t + 1, :] for n in range(1, 8)]
        top = functools.reduce(jnp.maximum, stats)
        shares = [jnp.exp2(s - top) for s in stats]
        scale = 1.0 / sum(shares)
        piece = [part_out[0, 64 * t : 64 * t + 64, :]] + [part_in[n, 64 * t : 64 * t + 64, :] for n in range(1, 8)]
        mixed.append(sum(p.astype(F32) * (s * scale) for p, s in zip(piece, shares)))
    back_out[...] = jnp.concatenate(mixed, axis=0).T.astype(BF16).reshape(8, 32, 128)

    returns = []
    for k in (4, 3, 5, 2, 6, 1, 7):
        copy = pltpu.make_async_remote_copy(
            src_ref=back_out.at[(y + k) % 8],
            dst_ref=back_in.at[y],
            send_sem=bk_s.at[k],
            recv_sem=bk_r.at[k],
            device_id=y_peer(k),
            device_id_type=MESH,
        )
        copy.start()
        returns.append(copy)
    back_in[y] = back_out[y]
    w_copy.wait()
    for copy in started:
        copy.wait_send()
    for n in range(1, 8):
        for copy in give_back(n):
            copy.wait_send()
    for copy in returns:
        copy.wait_recv()
    halves = [jnp.concatenate([back_in[h][:, 64 * t : 64 * t + 64] for h in range(8)], axis=1) for t in range(2)]
    out_ref[...] = dot(jnp.concatenate(halves, axis=0), w_vmem[...]).astype(BF16)
    for copy in returns:
        copy.wait_send()


def body(qkv, w_out):
    dma = pltpu.SemaphoreType.DMA
    return pl.pallas_call(
        kernel,
        out_shape=jax.ShapeDtypeStruct((64, 1024), BF16),
        in_specs=[pl.BlockSpec(memory_space=pltpu.VMEM), pl.BlockSpec(memory_space=pl.ANY)],
        out_specs=pl.BlockSpec(memory_space=pltpu.VMEM),
        scratch_shapes=[
            pltpu.VMEM((8, 3, 32, 128), BF16),
            pltpu.VMEM((3, 8, 32, 128), BF16),
            pltpu.VMEM((8, 256, 128), BF16),
            pltpu.VMEM((8, 2, 80, 256), BF16),
            pltpu.VMEM((8, 128, 256), BF16),
            pltpu.VMEM((16, 2, 128, 256), BF16),
            pltpu.VMEM((16, 80, 256), F32),
            pltpu.VMEM((16, 8, 256), F32),
            pltpu.VMEM((8, 128, 256), BF16),
            pltpu.VMEM((8, 8, 256), F32),
            pltpu.VMEM((8, 128, 256), BF16),
            pltpu.VMEM((8, 8, 256), F32),
            pltpu.VMEM((8, 32, 128), BF16),
            pltpu.VMEM((8, 32, 128), BF16),
            pltpu.VMEM((512, 1024), BF16),
            pltpu.VMEM((3, 64, 512), BF16),
            dma((8, 2)), dma((8, 2)),
            dma((4, 2, 2)), dma((8, 2)),
            dma((8,)), dma((8,)),
            dma((8, 2)), dma((8, 2)),
            dma((8,)), dma((8,)),
            dma,
        ],
        compiler_params=pltpu.CompilerParams(collective_id=0, has_side_effects=True, vmem_limit_bytes=56 << 20),
    )(qkv, w_out)


def solution(mesh):
    return jax.shard_map(
        body,
        mesh=mesh,
        in_specs=(P(("ctx", "head"), None, None), P()),
        out_specs=P(("ctx", "head"), None),
        check_vma=False,
    )
```

time: 402 us -> 62.1 us (0.15)
  waiting for transfers between devices: 216 us -> 0 us
  Pallas kernels: 0 us -> 58.2 us
  matrix products: 57.4 us -> 0 us
  other arithmetic: 51.3 us -> 0 us
  local copies, waits for them, and re-layouts: 35.2 us -> 3.36 us
  blocking collectives: 26.9 us -> 0 us
  between operations: 13.5 us -> 0.01 us
    all_gather x1 -> x0, waiting for transfers between devices: 216 us -> none  [body(): whole_kv = lax.all_gather(kv_local, 'ctx', axis=0, tiled=True)]
    pallas_call x0 -> x1, Pallas kernels: none -> 58.2 us  [body(): pl.pallas_call(kernel, out_shape=jax.ShapeDtypeStruct((64, 1024), BF16),...]
    dot_general x33 -> x0, matrix products: 57.4 us -> none  [the longest x16 43.3 us: attend_block(): jnp.einsum('fhd,khd->hfk', queries, keys_values[:, 0], preferred_element_...]
    reduce_sum x16 -> x0, other arithmetic: 49.5 us -> none  [attend_block(): totals = totals * factor + jnp.sum(weights, axis=2)]
    all_to_all x2 -> x0, blocking collectives: 26.9 us -> none  [the longest x1 15.7 us: body(): lax.all_to_all(spread_qkv, 'head', split_axis=2, concat_axis=0, tiled=True)]
    dynamic_slice x16 -> x0, local copies, waits for them, and re-layouts: 17.3 us -> none  [attend(): running, unused = lax.scan(step_fn, running, stacked)]
    reshape x3 -> x0, local copies, waits for them, and re-layouts: 9.84 us -> none  [the longest x1 8.26 us: attend(): stacked = kv_piece.reshape(key_count // 2048, 2048, kv_piece.shape[1])]
    while x48 -> x0, local copies, waits for them, and re-layouts: 5.3 us -> none
  transfers between devices with their start and end apart: 1 -> 0, of which waited for: 1 -> 0; matrix products, arithmetic and copies ran while one was open for 0% -> 0% of each run, Pallas kernels for 0% -> 0%
where the time goes in v1:
time: 62.1 us; the launch traced here: 61.6 us
  Pallas kernels  58.2 us (94%)
  local copies, waits for them, and re-layouts  3.36 us (5%)
    pallas_call x1, Pallas kernels, body(): pl.pallas_call(kernel, out_shape=jax.ShapeDtypeStruct((64, 1024), BF16),...  58.2 us
    unnamed x2, local copies, waits for them, and re-layouts  3.36 us

profile of v1, /device:TPU:1, one launch (start us, length us, event | category | flops | bytes accessed | tf_op | source)
XLA Modules:
  0.0 61.6 jit_solution(8476735625384658301)
XLA Ops:
  0.0 1.8 %copy.3.qkv_ref = bf16[64,3,512]{2,1,0:T(4,128)(2,1)} copy(bf16[64,3,512]{2,0,1:T(8,128)(2,1)} %param.2) | data formatting | bytes 393216 | tf_op args[0]
  1.8 58.2 %shard_map.28 = bf16[64,1024]{1,0:T(8,128)(2,1)} custom-call(bf16[64,3,512]{2,1,0:T(4,128)(2,1)} %copy.3.qkv_ref, bf16[512,1024]{1,0:T(8,128)(2,1)} %w_hbm.1), custom_call_target="tpu_custom_call" | custom-call | tf_op jit(solution)/shard_map/pallas_call | solution.py:288
  60.0 1.6 %copy.5 = bf16[64,1024]{1,0:T(8,128)(2,1)} copy(bf16[64,1024]{1,0:T(8,128)(2,1)} %shard_map.28) | data formatting | bytes 262144

commit v2 on v1

v2 whole, which is shorter than its diff:
```python
import functools

import jax
import jax.numpy as jnp
from jax import lax
from jax.experimental import pallas as pl
from jax.experimental.pallas import tpu as pltpu
from jax.sharding import PartitionSpec as P

MESH = pl.DeviceIdType.MESH
F32 = jnp.float32
BF16 = jnp.bfloat16
LOG2E = 1.4426950408889634

KEY_LEFT = ((0, 1), (1, 3), (3, 5), (5, 7))
KEY_RIGHT = ((0, 2), (2, 4), (4, 6), (6, 7))


def dot(a, b):
    return jnp.dot(a, b, preferred_element_type=F32)


def device(y, x, z, c):
    return ((y * 4 + x) * 2 + z // 4, (z % 4) * 2 + c)


def kernel(
    qkv_hbm, out_ref,
    qkv_ref, pieces, grouped, keys, doubled, values, queries, stationary, total, highest,
    part_out, stat_out, part_in, stat_in, back_out, back_in,
    a2a_s, a2a_r, kv_s, kv_r, q_s, q_r, po_s, po_r, bk_s, bk_r, in_sem,
):
    ctx, head = lax.axis_index("ctx"), lax.axis_index("head")
    y, x, z, c = ctx // 8, (ctx // 2) % 4, (ctx % 2) * 4 + head // 2, head % 2

    def y_peer(k):
        return device((y + k) % 8, x, z, c)

    def xc_peer(n):
        pair = n // 2
        dx = pair + pair // 2 - 2 * (pair // 3)
        return device(y, (x + dx) % 4, z, (c + n % 2) % 2)

    def inverse(n):
        pair = n // 2
        return 2 * ((2 * pair) % 3 + 3 * (pair // 3)) + n % 2

    left, right = device(y, x, (z + 7) % 8, c), device(y, x, (z + 1) % 8, c)

    barrier = pltpu.get_barrier_semaphore()
    partners = [y_peer(k) for k in range(1, 8)] + [xc_peer(n) for n in range(1, 8)] + [left, right]
    for partner in partners:
        pl.semaphore_signal(barrier, inc=1, device_id=partner, device_id_type=MESH)

    fetch = pltpu.make_async_copy(qkv_hbm, qkv_ref, in_sem)
    fetch.start()
    fetch.wait()

    for t in (1, 2, 0):
        for h in range(8):
            cut = qkv_ref[t, :, 64 * h : 64 * h + 64]
            pieces[h, t] = jnp.concatenate([cut[:32], cut[32:]], axis=1)

    pl.semaphore_wait(barrier, len(partners))

    def spread(k, first, count, part):
        there = (y + k) % 8
        return pltpu.make_async_remote_copy(
            src_ref=pieces.at[there, pl.ds(first, count)],
            dst_ref=grouped.at[pl.ds(first, count), y],
            send_sem=a2a_s.at[k, part],
            recv_sem=a2a_r.at[k, part],
            device_id=y_peer(k),
            device_id_type=MESH,
        )

    kv_spread = [spread(k, 1, 2, 0) for k in (4, 3, 5, 2, 6, 1, 7)]
    q_spread = [spread(k, 0, 1, 1) for k in (4, 3, 5, 2, 6, 1, 7)]
    for copy in kv_spread + q_spread:
        copy.start()
    for t in range(3):
        grouped[t, y] = pieces[y, t]
    for n in range(8):
        values[n, :, 64:80, :] = jnp.ones((2, 16, 256), BF16)
    started = kv_spread + q_spread

    def send_keys(step, part):
        copies = []
        for direction in range(2):
            if step < 3 or direction == part:
                here, there = (KEY_LEFT, KEY_RIGHT)[direction][step]
                ref = (keys, values)[part]
                place = (lambda n: ref.at[n]) if part == 0 else (lambda n: ref.at[n, :, pl.ds(0, 64)])
                copies.append(
                    pltpu.make_async_remote_copy(
                        src_ref=place(here),
                        dst_ref=place(there),
                        send_sem=kv_s.at[step, direction, part],
                        recv_sem=kv_r.at[there, part],
                        device_id=(left, right)[direction],
                        device_id_type=MESH,
                    )
                )
        for copy in copies:
            copy.start()
        started.extend(copies)
        arriving[step, part] = copies

    arriving = {}

    def double_keys(n):
        both = keys[n]
        for h in range(2):
            one = both[:, 64 * h : 64 * h + 64]
            doubled[n, h] = jnp.concatenate([one, one], axis=1)

    def take_keys(step, part):
        for copy in arriving[step, part]:
            copy.wait_recv()
        if step < 3:
            send_keys(step + 1, part)
        if part == 0:
            for n in (1 + 2 * step, 2 + 2 * step)[: 2 if step < 3 else 1]:
                double_keys(n)

    for copy in kv_spread:
        copy.wait_recv()
    keys[0] = grouped[1].reshape(256, 128)
    send_keys(0, 0)
    turned = grouped[2].reshape(256, 128).astype(F32).T.astype(BF16)
    values[0, 0, :64] = turned[:64]
    values[0, 1, :64] = turned[64:]
    send_keys(0, 1)
    double_keys(0)

    for copy in q_spread:
        copy.wait_recv()
    queries[0] = grouped[0].reshape(256, 128).astype(F32).T.astype(BF16)

    q_copies = {}
    for n in (1, 2, 4, 3, 5, 6, 7):
        q_copies[n] = pltpu.make_async_remote_copy(
            src_ref=queries.at[0],
            dst_ref=queries.at[inverse(n)],
            send_sem=q_s.at[n],
            recv_sem=q_r.at[inverse(n)],
            device_id=xc_peer(n),
            device_id_type=MESH,
        )
        q_copies[n].start()
        started.append(q_copies[n])

    def take_queries(n):
        if n:
            q_copies[inverse(n)].wait_recv()
        scaled = queries[n].astype(F32) * (LOG2E / 8)
        high = scaled.astype(BF16)
        low = (scaled - high.astype(F32)).astype(BF16)
        for t in range(2):
            stationary[2 * n + t, :64, :] = high[64 * t : 64 * t + 64]
            stationary[2 * n + t, 64:, :] = low[64 * t : 64 * t + 64]

    def scores(i, n, h):
        found = [dot(doubled[n, h], stationary[2 * i + t]) for t in range(2)]
        return found, [jnp.max(s.reshape(32, 8, 256), axis=0) for s in found]

    def weigh(i, n, h, found, top):
        for t in range(2):
            newest = jnp.max(top[t], axis=0, keepdims=True)
            first = n == 0 and h == 0
            if not first:
                before = highest[2 * i + t][:1]
                newest = jnp.maximum(before, newest)
                factor = jnp.exp2(before - newest)
            highest[2 * i + t] = jnp.broadcast_to(newest, (8, 256))
            added = dot(values[n, h], jnp.exp2(found[t] - newest).astype(BF16))
            total[2 * i + t] = added if first else total[2 * i + t] * factor + added

    def attend(chunks, slots):
        held = []
        for i in chunks:
            for n in slots:
                for h in range(2):
                    held.append((i, n, h, *scores(i, n, h)))
                    if len(held) > 2:
                        weigh(*held.pop(0))
        for unit in held:
            weigh(*unit)

    take_queries(0)
    attend((0,), (0,))
    take_queries(1)
    attend((1,), (0,))
    take_keys(0, 0)
    take_keys(0, 1)
    attend((0, 1), (1, 2))
    take_queries(2)
    take_queries(4)
    attend((2, 4), (0, 1, 2))
    take_keys(1, 0)
    take_queries(3)
    take_queries(5)
    take_keys(1, 1)
    attend((3, 5), (0, 1, 2))

    attend((0, 1, 2, 3), (3, 4))
    take_keys(2, 0)
    take_queries(6)
    take_queries(7)
    attend((4, 5), (3, 4))
    take_keys(2, 1)
    attend((6, 7), (0, 1, 2, 3, 4))
    take_keys(3, 0)
    take_keys(3, 1)

    def give_back(n):
        there = inverse(n)
        pairs = ((part_out, part_in), (stat_out, stat_in))
        return [
            pltpu.make_async_remote_copy(
                src_ref=mine.at[n],
                dst_ref=theirs.at[there],
                send_sem=po_s.at[n, k],
                recv_sem=po_r.at[there, k],
                device_id=xc_peer(n),
                device_id_type=MESH,
            )
            for k, (mine, theirs) in enumerate(pairs)
        ]

    @pl.loop(0, 4)
    def _(k):
        first = 6 - 2 * k
        attend((first, first + 1), (5, 6, 7))
        for i in (first, first + 1):
            for t in range(2):
                whole = total[2 * i + t]
                sums = whole[64:65]
                part_out[i, 64 * t : 64 * t + 64, :] = (whole[:64] * (1.0 / sums)).astype(BF16)
                stat_out[i, 4 * t : 4 * t + 4, :] = jnp.broadcast_to(highest[2 * i + t][:1] + jnp.log2(sums), (4, 256))

            @pl.when(i != 0)
            def _():
                for copy in give_back(i):
                    copy.start()

    for n in range(1, 8):
        for copy in give_back(inverse(n)):
            copy.wait_recv()
    mixed = []
    for t in range(2):
        stats = [stat_out[0, 4 * t : 4 * t + 1, :]] + [stat_in[n, 4 * t : 4 * t + 1, :] for n in range(1, 8)]
        top = functools.reduce(jnp.maximum, stats)
        shares = [jnp.exp2(s - top) for s in stats]
        scale = 1.0 / sum(shares)
        piece = [part_out[0, 64 * t : 64 * t + 64, :]] + [part_in[n, 64 * t : 64 * t + 64, :] for n in range(1, 8)]
        mixed.append(sum(p.astype(F32) * (s * scale) for p, s in zip(piece, shares)))
    back_out[...] = jnp.concatenate(mixed, axis=0).T.astype(BF16).reshape(8, 32, 128)

    returns = []
    for k in (4, 3, 5, 2, 6, 1, 7):
        copy = pltpu.make_async_remote_copy(
            src_ref=back_out.at[(y + k) % 8],
            dst_ref=back_in.at[y],
            send_sem=bk_s.at[k],
            recv_sem=bk_r.at[k],
            device_id=y_peer(k),
            device_id_type=MESH,
        )
        copy.start()
        returns.append(copy)
    back_in[y] = back_out[y]
    for copy in started:
        copy.wait_send()
    for n in range(1, 8):
        for copy in give_back(n):
            copy.wait_send()
    for copy in returns:
        copy.wait_recv()
    for h in range(8):
        for t in range(2):
            out_ref[32 * t : 32 * t + 32, 64 * h : 64 * h + 64] = back_in[h][:, 64 * t : 64 * t + 64]
    for copy in returns:
        copy.wait_send()


def body(qkv, w_out):
    dma = pltpu.SemaphoreType.DMA
    attended = pl.pallas_call(
        kernel,
        out_shape=jax.ShapeDtypeStruct((64, 512), BF16),
        in_specs=[pl.BlockSpec(memory_space=pl.ANY)],
        out_specs=pl.BlockSpec(memory_space=pltpu.VMEM),
        scratch_shapes=[
            pltpu.VMEM((3, 64, 512), BF16),
            pltpu.VMEM((8, 3, 32, 128), BF16),
            pltpu.VMEM((3, 8, 32, 128), BF16),
            pltpu.VMEM((8, 256, 128), BF16),
            pltpu.VMEM((8, 2, 256, 128), BF16),
            pltpu.VMEM((8, 2, 80, 256), BF16),
            pltpu.VMEM((8, 128, 256), BF16),
            pltpu.VMEM((16, 128, 256), BF16),
            pltpu.VMEM((16, 80, 256), F32),
            pltpu.VMEM((16, 8, 256), F32),
            pltpu.VMEM((8, 128, 256), BF16),
            pltpu.VMEM((8, 8, 256), F32),
            pltpu.VMEM((8, 128, 256), BF16),
            pltpu.VMEM((8, 8, 256), F32),
            pltpu.VMEM((8, 32, 128), BF16),
            pltpu.VMEM((8, 32, 128), BF16),
            dma((8, 2)), dma((8, 2)),
            dma((4, 2, 2)), dma((8, 2)),
            dma((8,)), dma((8,)),
            dma((8, 2)), dma((8, 2)),
            dma((8,)), dma((8,)),
            dma,
        ],
        compiler_params=pltpu.CompilerParams(collective_id=0, has_side_effects=True, vmem_limit_bytes=56 << 20),
    )(qkv.transpose(1, 0, 2))
    return dot(attended, w_out).astype(BF16)


def solution(mesh):
    return jax.shard_map(
        body,
        mesh=mesh,
        in_specs=(P(("ctx", "head"), None, None), P()),
        out_specs=P(("ctx", "head"), None),
        check_vma=False,
    )
```

time: 62.1 us -> 57.5 us (0.926)
  local copies, waits for them, and re-layouts: 3.36 us -> 0.01 us
  Pallas kernels: 58.2 us -> 55.6 us
  matrix products: 0 us -> 1.8 us
    unnamed x2, local copies, waits for them, and re-layouts: 3.36 us -> 0.01 us
    pallas_call x1, Pallas kernels: 58.2 us -> 55.6 us  [body(): pl.pallas_call(kernel, out_shape=jax.ShapeDtypeStruct((64, 512), BF16), i...]
    dot_general x0 -> x1, matrix products: none -> 1.8 us  [dot(): return jnp.dot(a, b, preferred_element_type=F32)]
where the time goes in v2:
time: 57.5 us; the launch traced here: 57.4 us
  Pallas kernels  55.6 us (97%)
  matrix products  1.8 us (3%)
    pallas_call x1, Pallas kernels, body(): pl.pallas_call(kernel, out_shape=jax.ShapeDtypeStruct((64, 512), BF16), i...  55.6 us
    dot_general x1, matrix products, dot(): return jnp.dot(a, b, preferred_element_type=F32)  1.8 us

profile of v2, /device:TPU:1, one launch (start us, length us, event | category | flops | bytes accessed | tf_op | source)
XLA Modules:
  0.0 57.4 jit_solution(17507150498867467013)
XLA Ops:
  0.0 0.0 copy-start
  0.0 55.6 %shard_map.28 = bf16[64,512]{1,0:T(8,128)(2,1)} custom-call(bf16[3,64,512]{2,1,0:T(8,128)(2,1)} %bitcast.3), custom_call_target="tpu_custom_call" | custom-call | tf_op jit(solution)/shard_map/pallas_call | solution.py:289
  55.6 0.0 copy-done
  55.6 1.8 %convolution_convert_fusion = bf16[64,1024]{1,0:T(8,128)(2,1)} fusion(bf16[64,512]{1,0:T(8,128)(2,1)} %shard_map.28, bf16[512,1024]{1,0:T(8,128)(2,1)S(1)} %copy-done), kind=kOutput, calls=%fused_computation | convolution fusion | flops 67174400 | bytes 1245184 | tf_op jit(solution)/shard_map/dot_general | solution.py:20
Async XLA Ops:
  0.0 55.6 %copy-start = (bf16[512,1024]{1,0:T(8,128)(2,1)S(1)}, bf16[512,1024]{1,0:T(8,128)(2,1)}, u32[]{:S(2)}) copy-start(bf16[512,1024]{1,0:T(8,128)(2,1)} %param.3) | copy-start | bytes 3145732

commit v3 on v2

--- a/solution.py
+++ b/solution.py
@@ -84,17 +84,20 @@
         values[n, :, 64:80, :] = jnp.ones((2, 16, 256), BF16)
     started = kv_spread + q_spread
 
+    def place(n, part):
+        if part < 2:
+            return keys.at[n, pl.ds(128 * part, 128)]
+        return values.at[n, part - 2, pl.ds(0, 64)]
+
     def send_keys(step, part):
         copies = []
         for direction in range(2):
-            if step < 3 or direction == part:
+            if step < 3 or direction == part // 2:
                 here, there = (KEY_LEFT, KEY_RIGHT)[direction][step]
-                ref = (keys, values)[part]
-                place = (lambda n: ref.at[n]) if part == 0 else (lambda n: ref.at[n, :, pl.ds(0, 64)])
                 copies.append(
                     pltpu.make_async_remote_copy(
-                        src_ref=place(here),
-                        dst_ref=place(there),
+                        src_ref=place(here, part),
+                        dst_ref=place(there, part),
                         send_sem=kv_s.at[step, direction, part],
                         recv_sem=kv_r.at[there, part],
                         device_id=(left, right)[direction],
@@ -108,30 +111,35 @@
 
     arriving = {}
 
-    def double_keys(n):
-        both = keys[n]
+    def double_keys(n, part):
+        both = keys[n, 128 * part : 128 * part + 128]
         for h in range(2):
             one = both[:, 64 * h : 64 * h + 64]
-            doubled[n, h] = jnp.concatenate([one, one], axis=1)
-
-    def take_keys(step, part):
-        for copy in arriving[step, part]:
-            copy.wait_recv()
-        if step < 3:
-            send_keys(step + 1, part)
-        if part == 0:
-            for n in (1 + 2 * step, 2 + 2 * step)[: 2 if step < 3 else 1]:
-                double_keys(n)
+            doubled[n, h, 128 * part : 128 * part + 128] = jnp.concatenate([one, one], axis=1)
+
+    def take_keys(step, *parts):
+        for part in parts:
+            for copy in arriving[step, part]:
+                copy.wait_recv()
+            if step < 3:
+                send_keys(step + 1, part)
+        for part in parts:
+            if part < 2:
+                for n in (1 + 2 * step, 2 + 2 * step)[: 2 if step < 3 else 1]:
+                    double_keys(n, part)
 
     for copy in kv_spread:
         copy.wait_recv()
     keys[0] = grouped[1].reshape(256, 128)
     send_keys(0, 0)
+    send_keys(0, 1)
     turned = grouped[2].reshape(256, 128).astype(F32).T.astype(BF16)
     values[0, 0, :64] = turned[:64]
     values[0, 1, :64] = turned[64:]
-    send_keys(0, 1)
-    double_keys(0)
+    send_keys(0, 2)
+    send_keys(0, 3)
+    double_keys(0, 0)
+    double_keys(0, 1)
 
     for copy in q_spread:
         copy.wait_recv()
@@ -164,54 +172,47 @@
         found = [dot(doubled[n, h], stationary[2 * i + t]) for t in range(2)]
         return found, [jnp.max(s.reshape(32, 8, 256), axis=0) for s in found]
 
+    state = {"chunk": None}
+
+    def store():
+        if state["chunk"] is not None:
+            for t in range(2):
+                top, whole = state["values"][t]
+                highest[2 * state["chunk"] + t] = jnp.broadcast_to(top, (8, 256))
+                total[2 * state["chunk"] + t] = whole
+
+    def load(i, first):
+        store()
+        state["chunk"] = i
+        state["values"] = [None if first else (highest[2 * i + t][:1], total[2 * i + t]) for t in range(2)]
+
     def weigh(i, n, h, found, top):
+        if state["chunk"] != i:
+            load(i, n == 0 and h == 0)
         for t in range(2):
             newest = jnp.max(top[t], axis=0, keepdims=True)
-            first = n == 0 and h == 0
-            if not first:
-                before = highest[2 * i + t][:1]
+            if state["values"][t] is not None:
+                before, whole = state["values"][t]
                 newest = jnp.maximum(before, newest)
                 factor = jnp.exp2(before - newest)
-            highest[2 * i + t] = jnp.broadcast_to(newest, (8, 256))
             added = dot(values[n, h], jnp.exp2(found[t] - newest).astype(BF16))
-            total[2 * i + t] = added if first else total[2 * i + t] * factor + added
+            state["values"][t] = (newest, added if state["values"][t] is None else whole * factor + added)
+        if n == 7 and h == 1:
+            give(i)
+
+    held = []
 
     def attend(chunks, slots):
-        held = []
         for i in chunks:
             for n in slots:
                 for h in range(2):
                     held.append((i, n, h, *scores(i, n, h)))
                     if len(held) > 2:
                         weigh(*held.pop(0))
-        for unit in held:
-            weigh(*unit)
-
-    take_queries(0)
-    attend((0,), (0,))
-    take_queries(1)
-    attend((1,), (0,))
-    take_keys(0, 0)
-    take_keys(0, 1)
-    attend((0, 1), (1, 2))
-    take_queries(2)
-    take_queries(4)
-    attend((2, 4), (0, 1, 2))
-    take_keys(1, 0)
-    take_queries(3)
-    take_queries(5)
-    take_keys(1, 1)
-    attend((3, 5), (0, 1, 2))
-
-    attend((0, 1, 2, 3), (3, 4))
-    take_keys(2, 0)
-    take_queries(6)
-    take_queries(7)
-    attend((4, 5), (3, 4))
-    take_keys(2, 1)
-    attend((6, 7), (0, 1, 2, 3, 4))
-    take_keys(3, 0)
-    take_keys(3, 1)
+
+    def finish_units():
+        while held:
+            weigh(*held.pop(0))
 
     def give_back(n):
         there = inverse(n)
@@ -228,21 +229,49 @@
             for k, (mine, theirs) in enumerate(pairs)
         ]
 
-    @pl.loop(0, 4)
-    def _(k):
-        first = 6 - 2 * k
-        attend((first, first + 1), (5, 6, 7))
-        for i in (first, first + 1):
-            for t in range(2):
-                whole = total[2 * i + t]
-                sums = whole[64:65]
-                part_out[i, 64 * t : 64 * t + 64, :] = (whole[:64] * (1.0 / sums)).astype(BF16)
-                stat_out[i, 4 * t : 4 * t + 4, :] = jnp.broadcast_to(highest[2 * i + t][:1] + jnp.log2(sums), (4, 256))
-
-            @pl.when(i != 0)
-            def _():
-                for copy in give_back(i):
-                    copy.start()
+    def give(i):
+        for t in range(2):
+            top, whole = state["values"][t]
+            sums = whole[64:65]
+            part_out[i, 64 * t : 64 * t + 64, :] = (whole[:64] * (1.0 / sums)).astype(BF16)
+            stat_out[i, 4 * t : 4 * t + 4, :] = jnp.broadcast_to(top + jnp.log2(sums), (4, 256))
+        state["chunk"] = None
+        if i:
+            for copy in give_back(i):
+                copy.start()
+
+    take_queries(0)
+    attend((0,), (0,))
+    take_queries(1)
+    attend((1,), (0,))
+    take_keys(0, 0, 1, 2, 3)
+    attend((0, 1), (1, 2))
+    take_queries(2)
+    take_queries(4)
+    take_keys(1, 0)
+    attend((2,), (0, 1, 2))
+    take_keys(1, 1)
+    attend((4,), (0, 1, 2))
+    take_queries(3)
+    take_queries(5)
+    take_keys(1, 2)
+    attend((3,), (0, 1, 2))
+    take_keys(1, 3)
+    attend((5,), (0, 1, 2))
+    take_keys(2, 0)
+    attend((0, 1), (3, 4))
+    take_keys(2, 1)
+    attend((2,), (3, 4))
+    take_keys(2, 2)
+    attend((3, 4), (3, 4))
+    take_keys(2, 3)
+    attend((5,), (3, 4))
+    take_queries(6)
+    take_queries(7)
+    attend((6, 7), (0, 1, 2, 3, 4))
+    take_keys(3, 0, 1, 2, 3)
+    attend((6, 7, 2, 4, 3, 5, 0, 1), (5, 6, 7))
+    finish_units()
 
     for n in range(1, 8):
         for copy in give_back(inverse(n)):
@@ -309,7 +338,7 @@
             pltpu.VMEM((8, 32, 128), BF16),
             pltpu.VMEM((8, 32, 128), BF16),
             dma((8, 2)), dma((8, 2)),
-            dma((4, 2, 2)), dma((8, 2)),
+            dma((4, 2, 4)), dma((8, 4)),
             dma((8,)), dma((8,)),
             dma((8, 2)), dma((8, 2)),
             dma((8,)), dma((8,)),

time: 57.5 us -> 55.5 us (0.965)
  Pallas kernels: 55.6 us -> 53.5 us
    pallas_call x1, Pallas kernels: 55.6 us -> 53.5 us  [body(): pl.pallas_call(kernel, out_shape=jax.ShapeDtypeStruct((64, 512), BF16), i...]
where the time goes in v3:
time: 55.5 us; the launch traced here: 55.3 us
  Pallas kernels  53.5 us (96%)
  matrix products  1.8 us (3%)
    pallas_call x1, Pallas kernels, body(): pl.pallas_call(kernel, out_shape=jax.ShapeDtypeStruct((64, 512), BF16), i...  53.5 us
    dot_general x1, matrix products, dot(): return jnp.dot(a, b, preferred_element_type=F32)  1.8 us

profile of v3, /device:TPU:1, one launch (start us, length us, event | category | flops | bytes accessed | tf_op | source)
XLA Modules:
  0.0 55.3 jit_solution(6505093342154720971)
XLA Ops:
  0.0 0.0 copy-start
  0.0 53.5 %shard_map.28 = bf16[64,512]{1,0:T(8,128)(2,1)} custom-call(bf16[3,64,512]{2,1,0:T(8,128)(2,1)} %bitcast.3), custom_call_target="tpu_custom_call" | custom-call | tf_op jit(solution)/shard_map/pallas_call | solution.py:318
  53.5 0.0 copy-done
  53.5 1.8 %convolution_convert_fusion = bf16[64,1024]{1,0:T(8,128)(2,1)} fusion(bf16[64,512]{1,0:T(8,128)(2,1)} %shard_map.28, bf16[512,1024]{1,0:T(8,128)(2,1)S(1)} %copy-done), kind=kOutput, calls=%fused_computation | convolution fusion | flops 67174400 | bytes 1245184 | tf_op jit(solution)/shard_map/dot_general | solution.py:20
Async XLA Ops:
  0.0 53.5 %copy-start = (bf16[512,1024]{1,0:T(8,128)(2,1)S(1)}, bf16[512,1024]{1,0:T(8,128)(2,1)}, u32[]{:S(2)}) copy-start(bf16[512,1024]{1,0:T(8,128)(2,1)} %param.3) | copy-start | bytes 3145732

commit v4 on v3

--- a/solution.py
+++ b/solution.py
@@ -89,9 +89,9 @@
             return keys.at[n, pl.ds(128 * part, 128)]
         return values.at[n, part - 2, pl.ds(0, 64)]
 
-    def send_keys(step, part):
+    def send_keys(step, part, *directions):
         copies = []
-        for direction in range(2):
+        for direction in directions:
             if step < 3 or direction == part // 2:
                 here, there = (KEY_LEFT, KEY_RIGHT)[direction][step]
                 copies.append(
@@ -107,7 +107,7 @@
         for copy in copies:
             copy.start()
         started.extend(copies)
-        arriving[step, part] = copies
+        arriving[step, part] = arriving.get((step, part), []) + copies
 
     arriving = {}
 
@@ -119,10 +119,10 @@
 
     def take_keys(step, *parts):
         for part in parts:
-            for copy in arriving[step, part]:
+            for direction, copy in enumerate(arriving[step, part]):
                 copy.wait_recv()
-            if step < 3:
-                send_keys(step + 1, part)
+                if step < 3:
+                    send_keys(step + 1, part, direction)
         for part in parts:
             if part < 2:
                 for n in (1 + 2 * step, 2 + 2 * step)[: 2 if step < 3 else 1]:
@@ -131,13 +131,13 @@
     for copy in kv_spread:
         copy.wait_recv()
     keys[0] = grouped[1].reshape(256, 128)
-    send_keys(0, 0)
-    send_keys(0, 1)
+    send_keys(0, 0, 0, 1)
+    send_keys(0, 1, 0, 1)
     turned = grouped[2].reshape(256, 128).astype(F32).T.astype(BF16)
     values[0, 0, :64] = turned[:64]
     values[0, 1, :64] = turned[64:]
-    send_keys(0, 2)
-    send_keys(0, 3)
+    send_keys(0, 2, 0, 1)
+    send_keys(0, 3, 0, 1)
     double_keys(0, 0)
     double_keys(0, 1)
 
@@ -234,7 +234,10 @@
             top, whole = state["values"][t]
             sums = whole[64:65]
             part_out[i, 64 * t : 64 * t + 64, :] = (whole[:64] * (1.0 / sums)).astype(BF16)
-            stat_out[i, 4 * t : 4 * t + 4, :] = jnp.broadcast_to(top + jnp.log2(sums), (4, 256))
+            stat = top + jnp.log2(sums)
+            for k in range(2):
+                row = 4 * t + 2 * k
+                stat_out[i, row : row + 2, :] = jnp.broadcast_to(stat[:, 128 * k : 128 * k + 128], (2, 128))
         state["chunk"] = None
         if i:
             for copy in give_back(i):
@@ -278,7 +281,10 @@
             copy.wait_recv()
     mixed = []
     for t in range(2):
-        stats = [stat_out[0, 4 * t : 4 * t + 1, :]] + [stat_in[n, 4 * t : 4 * t + 1, :] for n in range(1, 8)]
+        stats = [
+            jnp.concatenate([ref[n, 4 * t + 2 * k : 4 * t + 2 * k + 1, :] for k in range(2)], axis=1)
+            for n, ref in enumerate([stat_out] + 7 * [stat_in])
+        ]
         top = functools.reduce(jnp.maximum, stats)
         shares = [jnp.exp2(s - top) for s in stats]
         scale = 1.0 / sum(shares)
@@ -332,9 +338,9 @@
             pltpu.VMEM((16, 80, 256), F32),
             pltpu.VMEM((16, 8, 256), F32),
             pltpu.VMEM((8, 128, 256), BF16),
-            pltpu.VMEM((8, 8, 256), F32),
+            pltpu.VMEM((8, 8, 128), F32),
             pltpu.VMEM((8, 128, 256), BF16),
-            pltpu.VMEM((8, 8, 256), F32),
+            pltpu.VMEM((8, 8, 128), F32),
             pltpu.VMEM((8, 32, 128), BF16),
             pltpu.VMEM((8, 32, 128), BF16),
             dma((8, 2)), dma((8, 2)),

time: 55.5 us -> 55.1 us (level)
  no operation moved by 1% of the time
where the time goes in v4:
time: 55.1 us; the launch traced here: 55 us
  Pallas kernels  53.2 us (97%)
  matrix products  1.8 us (3%)
    pallas_call x1, Pallas kernels, body(): pl.pallas_call(kernel, out_shape=jax.ShapeDtypeStruct((64, 512), BF16), i...  53.2 us
    dot_general x1, matrix products, dot(): return jnp.dot(a, b, preferred_element_type=F32)  1.8 us

profile of v4, /device:TPU:1, one launch (start us, length us, event | category | flops | bytes accessed | tf_op | source)
XLA Modules:
  0.0 55.0 jit_solution(13763144013266939889)
XLA Ops:
  0.0 0.0 copy-start
  0.0 53.2 %shard_map.28 = bf16[64,512]{1,0:T(8,128)(2,1)} custom-call(bf16[3,64,512]{2,1,0:T(8,128)(2,1)} %bitcast.3), custom_call_target="tpu_custom_call" | custom-call | tf_op jit(solution)/shard_map/pallas_call | solution.py:324
  53.2 0.0 copy-done
  53.2 1.8 %convolution_convert_fusion = bf16[64,1024]{1,0:T(8,128)(2,1)} fusion(bf16[64,512]{1,0:T(8,128)(2,1)} %shard_map.28, bf16[512,1024]{1,0:T(8,128)(2,1)S(1)} %copy-done), kind=kOutput, calls=%fused_computation | convolution fusion | flops 67174400 | bytes 1245184 | tf_op jit(solution)/shard_map/dot_general | solution.py:20
Async XLA Ops:
  0.0 53.2 %copy-start = (bf16[512,1024]{1,0:T(8,128)(2,1)S(1)}, bf16[512,1024]{1,0:T(8,128)(2,1)}, u32[]{:S(2)}) copy-start(bf16[512,1024]{1,0:T(8,128)(2,1)} %param.3) | copy-start | bytes 3145732

commit v5 on v4

--- a/solution.py
+++ b/solution.py
@@ -56,11 +56,13 @@
     fetch.start()
     fetch.wait()
 
-    for t in (1, 2, 0):
+    def cut_pieces(t):
         for h in range(8):
             cut = qkv_ref[t, :, 64 * h : 64 * h + 64]
             pieces[h, t] = jnp.concatenate([cut[:32], cut[32:]], axis=1)
 
+    cut_pieces(1)
+    cut_pieces(2)
     pl.semaphore_wait(barrier, len(partners))
 
     def spread(k, first, count, part):
@@ -76,7 +78,10 @@
 
     kv_spread = [spread(k, 1, 2, 0) for k in (4, 3, 5, 2, 6, 1, 7)]
     q_spread = [spread(k, 0, 1, 1) for k in (4, 3, 5, 2, 6, 1, 7)]
-    for copy in kv_spread + q_spread:
+    for copy in kv_spread:
+        copy.start()
+    cut_pieces(0)
+    for copy in q_spread:
         copy.start()
     for t in range(3):
         grouped[t, y] = pieces[y, t]
@@ -276,20 +281,23 @@
     attend((6, 7, 2, 4, 3, 5, 0, 1), (5, 6, 7))
     finish_units()
 
-    for n in range(1, 8):
-        for copy in give_back(inverse(n)):
-            copy.wait_recv()
-    mixed = []
-    for t in range(2):
-        stats = [
-            jnp.concatenate([ref[n, 4 * t + 2 * k : 4 * t + 2 * k + 1, :] for k in range(2)], axis=1)
-            for n, ref in enumerate([stat_out] + 7 * [stat_in])
-        ]
-        top = functools.reduce(jnp.maximum, stats)
-        shares = [jnp.exp2(s - top) for s in stats]
-        scale = 1.0 / sum(shares)
-        piece = [part_out[0, 64 * t : 64 * t + 64, :]] + [part_in[n, 64 * t : 64 * t + 64, :] for n in range(1, 8)]
-        mixed.append(sum(p.astype(F32) * (s * scale) for p, s in zip(piece, shares)))
+    merged = []
+    for n in (0, 1, 6, 7, 4, 2, 5, 3):
+        if n:
+            for copy in give_back(inverse(n)):
+                copy.wait_recv()
+        part, stat = (part_in, stat_in) if n else (part_out, stat_out)
+        for t in range(2):
+            size = jnp.concatenate([stat[n, 4 * t + 2 * k : 4 * t + 2 * k + 1, :] for k in range(2)], axis=1)
+            piece = part[n, 64 * t : 64 * t + 64, :].astype(F32)
+            if n == 0:
+                merged.append((size, jnp.ones_like(size), piece))
+            else:
+                top, share, whole = merged[t]
+                newest = jnp.maximum(top, size)
+                old, new = jnp.exp2(top - newest), jnp.exp2(size - newest)
+                merged[t] = (newest, share * old + new, whole * old + piece * new)
+    mixed = [whole * (1.0 / share) for top, share, whole in merged]
     back_out[...] = jnp.concatenate(mixed, axis=0).T.astype(BF16).reshape(8, 32, 128)
 
     returns = []

time: 55.1 us -> 55.1 us (level)
  no operation moved by 1% of the time
where the time goes in v5:
time: 55.1 us; the launch traced here: 54.9 us
  Pallas kernels  53.1 us (96%)
  matrix products  1.8 us (3%)
    pallas_call x1, Pallas kernels, body(): pl.pallas_call(kernel, out_shape=jax.ShapeDtypeStruct((64, 512), BF16), i...  53.1 us
    dot_general x1, matrix products, dot(): return jnp.dot(a, b, preferred_element_type=F32)  1.8 us

profile of v5, /device:TPU:1, one launch (start us, length us, event | category | flops | bytes accessed | tf_op | source)
XLA Modules:
  0.0 54.9 jit_solution(15093317400856105625)
XLA Ops:
  0.0 0.0 copy-start
  0.0 53.1 %shard_map.28 = bf16[64,512]{1,0:T(8,128)(2,1)} custom-call(bf16[3,64,512]{2,1,0:T(8,128)(2,1)} %bitcast.3), custom_call_target="tpu_custom_call" | custom-call | tf_op jit(solution)/shard_map/pallas_call | solution.py:332
  53.1 0.0 copy-done
  53.1 1.8 %convolution_convert_fusion = bf16[64,1024]{1,0:T(8,128)(2,1)} fusion(bf16[64,512]{1,0:T(8,128)(2,1)} %shard_map.28, bf16[512,1024]{1,0:T(8,128)(2,1)S(1)} %copy-done), kind=kOutput, calls=%fused_computation | convolution fusion | flops 67174400 | bytes 1245184 | tf_op jit(solution)/shard_map/dot_general | solution.py:20
Async XLA Ops:
  0.0 53.1 %copy-start = (bf16[512,1024]{1,0:T(8,128)(2,1)S(1)}, bf16[512,1024]{1,0:T(8,128)(2,1)}, u32[]{:S(2)}) copy-start(bf16[512,1024]{1,0:T(8,128)(2,1)} %param.3) | copy-start | bytes 3145732

commit v6 on v5

--- a/solution.py
+++ b/solution.py
@@ -76,9 +76,10 @@
             device_id_type=MESH,
         )
 
-    kv_spread = [spread(k, 1, 2, 0) for k in (4, 3, 5, 2, 6, 1, 7)]
+    k_spread = [spread(k, 1, 1, 0) for k in (4, 3, 5, 2, 6, 1, 7)]
+    v_spread = [spread(k, 2, 1, 2) for k in (4, 3, 5, 2, 6, 1, 7)]
     q_spread = [spread(k, 0, 1, 1) for k in (4, 3, 5, 2, 6, 1, 7)]
-    for copy in kv_spread:
+    for copy in k_spread + v_spread:
         copy.start()
     cut_pieces(0)
     for copy in q_spread:
@@ -87,7 +88,7 @@
         grouped[t, y] = pieces[y, t]
     for n in range(8):
         values[n, :, 64:80, :] = jnp.ones((2, 16, 256), BF16)
-    started = kv_spread + q_spread
+    started = k_spread + v_spread + q_spread
 
     def place(n, part):
         if part < 2:
@@ -133,11 +134,13 @@
                 for n in (1 + 2 * step, 2 + 2 * step)[: 2 if step < 3 else 1]:
                     double_keys(n, part)
 
-    for copy in kv_spread:
+    for copy in k_spread:
         copy.wait_recv()
     keys[0] = grouped[1].reshape(256, 128)
     send_keys(0, 0, 0, 1)
     send_keys(0, 1, 0, 1)
+    for copy in v_spread:
+        copy.wait_recv()
     turned = grouped[2].reshape(256, 128).astype(F32).T.astype(BF16)
     values[0, 0, :64] = turned[:64]
     values[0, 1, :64] = turned[64:]
@@ -351,7 +354,7 @@
             pltpu.VMEM((8, 8, 128), F32),
             pltpu.VMEM((8, 32, 128), BF16),
             pltpu.VMEM((8, 32, 128), BF16),
-            dma((8, 2)), dma((8, 2)),
+            dma((8, 3)), dma((8, 3)),
             dma((4, 2, 4)), dma((8, 4)),
             dma((8,)), dma((8,)),
             dma((8, 2)), dma((8, 2)),

time: 55.1 us -> 55.2 us (level)
  no operation moved by 1% of the time
where the time goes in v6:
time: 55.2 us; the launch traced here: 55.1 us
  Pallas kernels  53.3 us (97%)
  matrix products  1.8 us (3%)
    pallas_call x1, Pallas kernels, body(): pl.pallas_call(kernel, out_shape=jax.ShapeDtypeStruct((64, 512), BF16), i...  53.3 us
    dot_general x1, matrix products, dot(): return jnp.dot(a, b, preferred_element_type=F32)  1.8 us

profile of v6, /device:TPU:1, one launch (start us, length us, event | category | flops | bytes accessed | tf_op | source)
XLA Modules:
  0.0 55.1 jit_solution(14666911478543478359)
XLA Ops:
  0.0 0.0 copy-start
  0.0 53.3 %shard_map.28 = bf16[64,512]{1,0:T(8,128)(2,1)} custom-call(bf16[3,64,512]{2,1,0:T(8,128)(2,1)} %bitcast.3), custom_call_target="tpu_custom_call" | custom-call | tf_op jit(solution)/shard_map/pallas_call | solution.py:335
  53.3 0.0 copy-done
  53.3 1.8 %convolution_convert_fusion = bf16[64,1024]{1,0:T(8,128)(2,1)} fusion(bf16[64,512]{1,0:T(8,128)(2,1)} %shard_map.28, bf16[512,1024]{1,0:T(8,128)(2,1)S(1)} %copy-done), kind=kOutput, calls=%fused_computation | convolution fusion | flops 67174400 | bytes 1245184 | tf_op jit(solution)/shard_map/dot_general | solution.py:20
Async XLA Ops:
  0.0 53.3 %copy-start = (bf16[512,1024]{1,0:T(8,128)(2,1)S(1)}, bf16[512,1024]{1,0:T(8,128)(2,1)}, u32[]{:S(2)}) copy-start(bf16[512,1024]{1,0:T(8,128)(2,1)} %param.3) | copy-start | bytes 3145732
